TPU v7x, 128 devices: a whole 4x4x4 slice. The times are simulated.
128 devices in a mesh: seg: 16 (over y, x), head: 8 (over z, core).
Axes of the slice: x: 4, y: 4, z: 4, core: 2. Of those that a mesh axis runs over, the one named last changes fastest.
Arguments:
- queries: bfloat16 [128, 256, 5120], P(('seg', 'head')), may hold values from -6 to 6
- key_states: bfloat16 [128, 256, 1024], P(('seg', 'head')), may hold values from -6 to 6
- values: bfloat16 [128, 256, 1024], P(('seg', 'head')), may hold values from -6 to 6
- grad_out: bfloat16 [128, 256, 5120], P(('seg', 'head')), may hold values from -6 to 6
- owners: int32 [128], replicated, may hold values from 0 to 127, as said below
- parents: int32 [128], replicated, may hold values from -1 to 31, as said below
- depths: int32 [128], replicated, may hold values from 0 to 2, as said below
- lengths: int32 [128], replicated, may hold values from 64 to 256, as said below
Outputs:
- query_grads: bfloat16 [128, 256, 5120], P(('seg', 'head'))
- key_grads: bfloat16 [128, 256, 1024], P(('seg', 'head'))
- value_grads: bfloat16 [128, 256, 1024], P(('seg', 'head'))
Inputs may be any that keep to these rules, and one draw needn't show every extreme that they name: A permutation: segment g sits in slot owners[g], on the index owners[g] // 8 of seg; each index of seg holds exactly 2 segments that have children. -1 exactly for the 8 roots, segments 0 to 7; any other segment's parent has a smaller number; segments 8 to 31 have roots as parents; every segment below 32 has a child and none from 32 on. `depths`: the number of ancestors: 0 for roots, else one more than the parent's. The first lengths[g] positions of a segment's slot are tokens, the rest padding.
All inputs are finite; a program needn't handle non-finite values.
Results may differ from a plain program's by a relative error of at most 0.014.
Values may be sent and summed in bfloat16 or wider, within the bound.
A program may use at most 128 MiB of HBM per device.

v0:
```python
import jax
import jax.numpy as jnp
from jax import lax
from jax.sharding import PartitionSpec as P

DH = 128
PUB = 2


def lookup(source_table, wanted):
    places = jnp.arange(source_table.shape[0], dtype=jnp.int32)
    picked = jnp.where(wanted[:, None] == places[None, :], source_table[None, :], 0)
    return jnp.sum(picked, axis=1)


def tree_tables(owners, parents, depths, lengths, per_device, published):
    count_all = owners.shape[0]
    slot_ids = jnp.arange(count_all, dtype=jnp.int32)
    segment_at = jnp.sum(
        jnp.where(owners[None, :] == slot_ids[:, None], slot_ids[None, :], 0), axis=1
    )
    first_up = lookup(parents, segment_at)
    second_up = lookup(parents, jnp.maximum(first_up, 0))
    levels = lookup(depths, segment_at)
    valid_one = (levels >= 1) & (first_up >= 0)
    valid_two = (levels >= 2) & valid_one & (second_up >= 0)
    slot_one = lookup(owners, jnp.maximum(first_up, 0))
    slot_two = lookup(owners, jnp.maximum(second_up, 0))
    own_length = lookup(lengths, segment_at)
    length_one = lookup(lengths, jnp.maximum(first_up, 0))
    length_two = lookup(lengths, jnp.maximum(second_up, 0))
    pointed = jnp.any(
        (slot_one[:, None] == slot_ids[None, :]) & valid_one[:, None]
        | (slot_two[:, None] == slot_ids[None, :]) & valid_two[:, None],
        axis=0,
    )
    device_of = slot_ids // per_device
    earlier = (
        (device_of[None, :] == device_of[:, None])
        & (slot_ids[None, :] < slot_ids[:, None])
        & pointed[None, :]
    )
    ranking = jnp.sum(earlier.astype(jnp.int32), axis=1)
    shared_index = device_of * published + ranking
    return (
        own_length,
        slot_one,
        slot_two,
        valid_one,
        valid_two,
        length_one,
        length_two,
        pointed,
        ranking,
        shared_index,
    )


def body(queries, key_states, values, grad_out, owners, parents, depths, lengths):
    query_all, grad_all, key_all, value_all = (
        lax.all_to_all(queries, "head", split_axis=2, concat_axis=0, tiled=True),
        lax.all_to_all(grad_out, "head", split_axis=2, concat_axis=0, tiled=True),
        lax.all_to_all(key_states, "head", split_axis=2, concat_axis=0, tiled=True),
        lax.all_to_all(values, "head", split_axis=2, concat_axis=0, tiled=True),
    )
    per_device, slot_size, query_width = query_all.shape
    kv_width = key_all.shape[2]
    kv_heads = kv_width // DH
    group_size = query_width // kv_width
    device_count = lax.axis_size("seg")
    first_row = lax.axis_index("seg") * per_device
    tables = tree_tables(owners, parents, depths, lengths, per_device, PUB)
    (
        own_length,
        slot_one,
        slot_two,
        valid_one,
        valid_two,
        length_one,
        length_two,
        pointed,
        ranking,
        shared_index,
    ) = tables
    index_one = lookup(shared_index, slot_one)
    index_two = lookup(shared_index, slot_two)

    def local_rows(source_table):
        return lax.dynamic_slice_in_dim(source_table, first_row, per_device)

    stacked = jnp.concatenate([key_all, value_all], axis=2)
    chosen = local_rows(pointed)[None, :] & (
        local_rows(ranking)[None, :] == jnp.arange(PUB, dtype=jnp.int32)[:, None]
    )
    publish = jnp.einsum(
        "pi,itc->ptc", chosen.astype(jnp.bfloat16), stacked, preferred_element_type=jnp.float32
    ).astype(jnp.bfloat16)
    shared = lax.all_gather(publish, "seg", axis=0, tiled=True)
    softmax_scale = DH ** (-0.5)
    rows = jnp.arange(slot_size, dtype=jnp.int32)
    columns = jnp.arange(3 * slot_size, dtype=jnp.int32)
    column_block = columns // slot_size
    column_inner = columns % slot_size

    def segment_grads(operands):
        (
            query_seg,
            grad_seg,
            stacked_seg,
            length_here,
            first_index,
            second_index,
            first_valid,
            second_valid,
            first_length,
            second_length,
        ) = operands
        ancestor_one = lax.dynamic_index_in_dim(shared, first_index, 0, keepdims=False)
        ancestor_two = lax.dynamic_index_in_dim(shared, second_index, 0, keepdims=False)
        key_value = jnp.concatenate([stacked_seg, ancestor_one, ancestor_two], axis=0)
        key_cat = key_value[:, :kv_width].reshape(3 * slot_size, kv_heads, DH)
        value_cat = key_value[:, kv_width:].reshape(3 * slot_size, kv_heads, DH)
        own_allowed = (column_inner[None, :] <= rows[:, None]) & (
            column_inner[None, :] < length_here
        )
        first_allowed = (column_inner[None, :] < first_length) & first_valid
        second_allowed = (column_inner[None, :] < second_length) & second_valid
        allowed = jnp.where(
            column_block[None, :] == 0,
            own_allowed,
            jnp.where(column_block[None, :] == 1, first_allowed, second_allowed),
        )
        live = rows < length_here
        gated = jnp.where(live[:, None], grad_seg, jnp.zeros_like(grad_seg)).reshape(
            slot_size, kv_heads, group_size, DH
        )
        query_heads = query_seg.reshape(slot_size, kv_heads, group_size, DH)
        scores = (
            jnp.einsum("tkgd,ukd->kgtu", query_heads, key_cat, preferred_element_type=jnp.float32)
            * softmax_scale
        )
        scores = jnp.where(allowed, scores, -1e30)
        highest = jnp.max(scores, axis=-1, keepdims=True)
        log_total = highest + jnp.log(jnp.sum(jnp.exp(scores - highest), axis=-1, keepdims=True))
        weights = jnp.exp(scores - log_total)
        weights_low = weights.astype(jnp.bfloat16)
        attended = jnp.einsum(
            "kgtu,ukd->tkgd", weights_low, value_cat, preferred_element_type=jnp.float32
        )
        deltas = jnp.sum(gated.astype(jnp.float32) * attended, axis=-1)
        weight_grads = jnp.einsum(
            "tkgd,ukd->kgtu", gated, value_cat, preferred_element_type=jnp.float32
        )
        score_low = (weights * (weight_grads - jnp.transpose(deltas, (1, 2, 0))[..., None])).astype(
            jnp.bfloat16
        )
        query_grads = softmax_scale * jnp.einsum(
            "kgtu,ukd->tkgd", score_low, key_cat, preferred_element_type=jnp.float32
        )
        query_grads = query_grads.astype(jnp.bfloat16).reshape(slot_size, query_width)
        key_part = softmax_scale * jnp.einsum(
            "kgtu,tkgd->ukd", score_low, query_heads, preferred_element_type=jnp.float32
        )
        value_part = jnp.einsum(
            "kgtu,tkgd->ukd", weights_low, gated, preferred_element_type=jnp.float32
        )
        both_grads = jnp.concatenate(
            [
                key_part.reshape(3 * slot_size, kv_width),
                value_part.reshape(3 * slot_size, kv_width),
            ],
            axis=1,
        )
        return (
            query_grads,
            both_grads[:slot_size],
            both_grads[slot_size:].reshape(2, slot_size, 2 * kv_width),
        )

    query_grads, own_terms, far_terms = lax.map(
        segment_grads,
        (
            query_all,
            grad_all,
            stacked,
            local_rows(own_length),
            local_rows(index_one),
            local_rows(index_two),
            local_rows(valid_one),
            local_rows(valid_two),
            local_rows(length_one),
            local_rows(length_two),
        ),
    )
    links_valid = jnp.stack([local_rows(valid_one), local_rows(valid_two)], axis=1).reshape(-1)
    links_index = jnp.stack([local_rows(index_one), local_rows(index_two)], axis=1).reshape(-1)
    targets = (
        (links_index[:, None] == jnp.arange(device_count * PUB, dtype=jnp.int32)[None, :])
        & links_valid[:, None]
    ).astype(jnp.float32)
    flattened = far_terms.reshape(per_device * 2, slot_size * 2 * kv_width)
    summed = jnp.dot(targets.T, flattened, precision=lax.Precision.HIGHEST)
    received = lax.psum_scatter(
        summed.reshape(PUB * lax.axis_size("seg"), slot_size, 2 * kv_width).astype(jnp.bfloat16),
        "seg",
        scatter_dimension=0,
        tiled=True,
    ).astype(jnp.float32)
    returned = jnp.einsum(
        "pi,ptc->itc", chosen.astype(jnp.float32), received, precision=lax.Precision.HIGHEST
    )
    totals = (own_terms + returned).astype(jnp.bfloat16)
    query_out, key_out, value_out = (
        lax.all_to_all(query_grads, "head", split_axis=0, concat_axis=2, tiled=True),
        lax.all_to_all(totals[:, :, :kv_width], "head", split_axis=0, concat_axis=2, tiled=True),
        lax.all_to_all(totals[:, :, kv_width:], "head", split_axis=0, concat_axis=2, tiled=True),
    )
    return (query_out, key_out, value_out)


def solution(mesh):
    placed = (
        P(("seg", "head"), None, None),
        P(("seg", "head"), None, None),
        P(("seg", "head"), None, None),
        P(("seg", "head"), None, None),
        P(),
        P(),
        P(),
        P(),
    )
    return jax.shard_map(
        body,
        mesh=mesh,
        in_specs=placed,
        out_specs=(
            P(("seg", "head"), None, None),
            P(("seg", "head"), None, None),
            P(("seg", "head"), None, None),
        ),
        check_vma=False,
    )
```

profile of v0, /device:TPU:1, one launch (start us, length us, event | category | flops | bytes accessed | tf_op | source)
XLA Modules:
  0.0 552.6 jit_solution(13793615365420855753)
XLA Ops:
  10.2 3.8 reduce.4
  15.0 6.8 %all-to-all-start = ((bf16[8,2,16384]{2,1,0:T(2,128)(2,1)}), bf16[8,2,16384]{2,1,0:T(2,128)(2,1)S(1)}, u32[]{:S(2)}, u32[]{:S(2)}) async-start(bf16[8,2,16384]{2,1,0:T(2,128)(2,1)} %reshape.243), calls=%async_computation | async-start | bytes 1048576 | tf_op jit(solution)/shard_map/all_to_all | solution.py:63
  31.3 4.3 all-to-all-start.1
  37.8 7.3 %all-to-all-done.1 = bf16[8,2,16384]{2,1,0:T(2,128)(2,1)S(1)} async-done(((bf16[8,2,16384]{2,1,0:T(2,128)(2,1)}), bf16[8,2,16384]{2,1,0:T(2,128)(2,1)S(1)}, u32[]{:S(2)}, u32[]{:S(2)}) %all-to-all-start.1) | async-done | bytes 524320 | tf_op jit(solution)/shard_map/all_to_all | solution.py:64
  49.2 8.2 %copy.112 = bf16[1,256,5120]{1,0,2:T(2,128)(2,1)} copy(bf16[1,256,5120]{2,1,0:T(8,128)(2,1)S(1)} %copy-done) | data formatting | bytes 5242880 | tf_op args[0]
  57.3 26.6 %reduce.5 = bf16[5120,256]{1,0:T(8,128)(2,1)S(1)} reduce(bf16[5120,1,256]{2,1,0:T(2,128)(2,1)} %bitcast.267, bf16[]{:T(256)} %broadcast.307), dimensions={1}, to_apply=%bitcast.170.reduce_sub_computation | reduce | bytes 5242882
  87.3 5.4 all-to-all-start.2
  92.7 8.2 %copy.113 = bf16[1,256,5120]{1,0,2:T(2,128)(2,1)} copy(bf16[1,256,5120]{2,1,0:T(8,128)(2,1)S(1)} %copy-done.1) | data formatting | bytes 5242880 | tf_op args[3]
  100.9 26.5 %reduce.6 = bf16[5120,256]{1,0:T(8,128)(2,1)S(1)} reduce(bf16[5120,1,256]{2,1,0:T(2,128)(2,1)} %bitcast.264, bf16[]{:T(256)} %broadcast.307), dimensions={1}, to_apply=%bitcast.172.reduce_sub_computation | reduce | bytes 5242882
  130.8 5.0 all-to-all-start.3
  139.5 7.3 %reshape.246 = bf16[5120,1,256]{2,1,0:T(2,128)(2,1)} reshape(bf16[8,2,81920]{2,1,0:T(2,128)(2,1)} %all-to-all-done.2) | data formatting | bytes 5242880
  146.8 4.4 copy.148
  151.2 16.5 %all-to-all-done.3 = bf16[8,2,81920]{2,1,0:T(2,128)(2,1)S(1)} async-done(((bf16[8,2,81920]{2,1,0:T(2,128)(2,1)}), bf16[8,2,81920]{2,1,0:T(2,128)(2,1)S(1)}, u32[]{:S(2)}, u32[]{:S(2)}) %all-to-all-start.3) | async-done | bytes 2621472 | tf_op jit(solution)/shard_map/all_to_all | solution.py:62
  167.7 4.8 reshape.248
  172.6 4.4 copy.149
  177.0 243.5 %while.16 = (s32[]{:T(128)}, bf16[8,256,640]{1,2,0:T(8,128)(2,1)}, f32[8,256,256]{2,0,1:T(8,128)}, f32[8,2,256,256]{3,2,1,0:T(8,128)}, bf16[8,256,256]{2,1,0:T(8...) while((s32[]{:T(128)}, bf16[8,256,640]{1,2,0:T(8,128)(2,1)}, ...), condition=%wide.region_17.18_spmd.clone.clone, body=%wide.region_13.17_spmd.clone.clone.sunk | while | flops 1533990656 | bytes 39727208 | solution.py:180
  199.0 6.9 %dynamic_update_slice.25 = f32[8,256,256]{2,0,1:T(8,128)} dynamic-update-slice(f32[8,256,256]{2,0,1:T(8,128)} %get-tuple-element.461, f32[1,256,256]{2,0,1:T(1,128)S(1)} %copy.166, s32[]{:T(128)S(6)} %copy.175, s32[]{:T(128)} %constant.92.clone.1..sunk, s32[]{:T(128)} %constant.92.clone.1..sunk) | dynamic-update-slice | bytes 524292 | tf_op jit(solution)/shard_map/while/body/jit(dynamic_update_index_in_dim)/dynamic_update_slice | solution.py:180
  229.4 6.9 %dynamic_update_slice.25 = f32[8,256,256]{2,0,1:T(8,128)} dynamic-update-slice(f32[8,256,256]{2,0,1:T(8,128)} %get-tuple-element.461, f32[1,256,256]{2,0,1:T(1,128)S(1)} %copy.166, s32[]{:T(128)S(6)} %copy.175, s32[]{:T(128)} %constant.92.clone.1..sunk, s32[]{:T(128)} %constant.92.clone.1..sunk) | dynamic-update-slice | bytes 524292 | tf_op jit(solution)/shard_map/while/body/jit(dynamic_update_index_in_dim)/dynamic_update_slice | solution.py:180
  259.8 6.9 %dynamic_update_slice.25 = f32[8,256,256]{2,0,1:T(8,128)} dynamic-update-slice(f32[8,256,256]{2,0,1:T(8,128)} %get-tuple-element.461, f32[1,256,256]{2,0,1:T(1,128)S(1)} %copy.166, s32[]{:T(128)S(6)} %copy.175, s32[]{:T(128)} %constant.92.clone.1..sunk, s32[]{:T(128)} %constant.92.clone.1..sunk) | dynamic-update-slice | bytes 524292 | tf_op jit(solution)/shard_map/while/body/jit(dynamic_update_index_in_dim)/dynamic_update_slice | solution.py:180
  290.2 6.9 %dynamic_update_slice.25 = f32[8,256,256]{2,0,1:T(8,128)} dynamic-update-slice(f32[8,256,256]{2,0,1:T(8,128)} %get-tuple-element.461, f32[1,256,256]{2,0,1:T(1,128)S(1)} %copy.166, s32[]{:T(128)S(6)} %copy.175, s32[]{:T(128)} %constant.92.clone.1..sunk, s32[]{:T(128)} %constant.92.clone.1..sunk) | dynamic-update-slice | bytes 524292 | tf_op jit(solution)/shard_map/while/body/jit(dynamic_update_index_in_dim)/dynamic_update_slice | solution.py:180
  320.7 6.9 %dynamic_update_slice.25 = f32[8,256,256]{2,0,1:T(8,128)} dynamic-update-slice(f32[8,256,256]{2,0,1:T(8,128)} %get-tuple-element.461, f32[1,256,256]{2,0,1:T(1,128)S(1)} %copy.166, s32[]{:T(128)S(6)} %copy.175, s32[]{:T(128)} %constant.92.clone.1..sunk, s32[]{:T(128)} %constant.92.clone.1..sunk) | dynamic-update-slice | bytes 524292 | tf_op jit(solution)/shard_map/while/body/jit(dynamic_update_index_in_dim)/dynamic_update_slice | solution.py:180
  351.1 6.9 %dynamic_update_slice.25 = f32[8,256,256]{2,0,1:T(8,128)} dynamic-update-slice(f32[8,256,256]{2,0,1:T(8,128)} %get-tuple-element.461, f32[1,256,256]{2,0,1:T(1,128)S(1)} %copy.166, s32[]{:T(128)S(6)} %copy.175, s32[]{:T(128)} %constant.92.clone.1..sunk, s32[]{:T(128)} %constant.92.clone.1..sunk) | dynamic-update-slice | bytes 524292 | tf_op jit(solution)/shard_map/while/body/jit(dynamic_update_index_in_dim)/dynamic_update_slice | solution.py:180
  381.5 6.9 %dynamic_update_slice.25 = f32[8,256,256]{2,0,1:T(8,128)} dynamic-update-slice(f32[8,256,256]{2,0,1:T(8,128)} %get-tuple-element.461, f32[1,256,256]{2,0,1:T(1,128)S(1)} %copy.166, s32[]{:T(128)S(6)} %copy.175, s32[]{:T(128)} %constant.92.clone.1..sunk, s32[]{:T(128)} %constant.92.clone.1..sunk) | dynamic-update-slice | bytes 524292 | tf_op jit(solution)/shard_map/while/body/jit(dynamic_update_index_in_dim)/dynamic_update_slice | solution.py:180
  412.0 6.9 %dynamic_update_slice.25 = f32[8,256,256]{2,0,1:T(8,128)} dynamic-update-slice(f32[8,256,256]{2,0,1:T(8,128)} %get-tuple-element.461, f32[1,256,256]{2,0,1:T(1,128)S(1)} %copy.166, s32[]{:T(128)S(6)} %copy.175, s32[]{:T(128)} %constant.92.clone.1..sunk, s32[]{:T(128)} %constant.92.clone.1..sunk) | dynamic-update-slice | bytes 524292 | tf_op jit(solution)/shard_map/while/body/jit(dynamic_update_index_in_dim)/dynamic_update_slice | solution.py:180
  420.5 8.2 %fusion.55 = bf16[32,256,256]{2,0,1:T(8,128)(2,1)S(1)} fusion(s32[16]{0:T(128)S(1)} %eq.83, pred[16]{0:T(512)(128)(4,1)S(1)} %and.162, f32[2,8,256,256]{3,2,1,0:T(8,128)} %bitcast.274), kind=kOutput, calls=%fused_computation.66 | convolution fusion | flops 404751360 | bytes 8388688 | tf_op jit(solution)/shard_map/dot_general | solution.py:202
  428.7 4.3 copy.120
  433.0 4.4 all-to-all-start.4
  437.5 71.3 %reduce-scatter.2.cloned.1.call-done = bf16[2,256,256]{2,1,0:T(8,128)(2,1)} async-done(((bf16[32,256,256]{2,1,0:T(8,128)(2,1)}), bf16[2,256,256]{2,1,0:T(8,128)(2,1)}) %reduce-scatter.2.cloned.1.call-update) | async-done | bytes 262160 | tf_op jit(solution)/shard_map/reduce_scatter | solution.py:203
  512.8 6.7 %all-to-all-start.6 = ((bf16[8,256,128]{2,1,0:T(8,128)(2,1)}), bf16[8,256,128]{2,1,0:T(8,128)(2,1)S(1)}, u32[]{:S(2)}, u32[]{:S(2)}) async-start(bf16[8,256,128]{2,1,0:T(8,128)(2,1)} %copy.125), calls=%async_computation.7 | async-start | bytes 1048576 | tf_op jit(solution)/shard_map/all_to_all | solution.py:216
  521.4 7.6 %all-to-all-done.6 = bf16[8,256,128]{2,1,0:T(8,128)(2,1)S(1)} async-done(((bf16[8,256,128]{2,1,0:T(8,128)(2,1)}), bf16[8,256,128]{2,1,0:T(8,128)(2,1)S(1)}, u32[]{:S(2)}, u32[]{:S(2)}) %all-to-all-start.6) | async-done | bytes 524320 | tf_op jit(solution)/shard_map/all_to_all | solution.py:216
  529.0 4.9 all-to-all-start.5
  537.9 5.6 %all-to-all-done.5 = bf16[8,256,128]{2,1,0:T(8,128)(2,1)} async-done(((bf16[8,256,128]{2,1,0:T(8,128)(2,1)}), bf16[8,256,128]{2,1,0:T(8,128)(2,1)}, u32[]{:S(2)}, u32[]{:S(2)}) %all-to-all-start.5) | async-done | bytes 524320 | tf_op jit(solution)/shard_map/all_to_all | solution.py:215
  (317 shorter events, 198.4 us)
Async XLA Ops:
  7.2 14.6 %copy-start.5 = (s32[128]{0:T(128)S(1)}, s32[128]{0:T(128)}, u32[]{:S(2)}) copy-start(s32[128]{0:T(128)} %param.14) | copy-start | bytes 1540
  7.2 14.7 %copy-start.7 = (s32[128]{0:T(128)S(1)}, s32[128]{0:T(128)}, u32[]{:S(2)}) copy-start(s32[128]{0:T(128)} %param.15) | copy-start | bytes 1540
  7.2 14.9 %copy-start.3 = (bf16[1,256,1024]{2,1,0:T(8,128)(2,1)S(1)}, bf16[1,256,1024]{2,1,0:T(8,128)(2,1)}, u32[]{:S(2)}) copy-start(bf16[1,256,1024]{2,1,0:T(8,128)(2,1)} %param.12) | copy-start | bytes 1572868
  10.2 17.7 %copy-start.4 = (s32[128]{0:T(128)S(1)}, s32[128]{0:T(128)}, u32[]{:S(2)}) copy-start(s32[128]{0:T(128)} %param.17) | copy-start | bytes 1540
  10.2 17.7 %copy-start.6 = (s32[128]{0:T(128)S(1)}, s32[128]{0:T(128)}, u32[]{:S(2)}) copy-start(s32[128]{0:T(128)} %param.16) | copy-start | bytes 1540
  15.0 16.3 %all-to-all-start = ((bf16[8,2,16384]{2,1,0:T(2,128)(2,1)}), bf16[8,2,16384]{2,1,0:T(2,128)(2,1)S(1)}, u32[]{:S(2)}, u32[]{:S(2)}) async-start(bf16[8,2,16384]{2,1,0:T(2,128)(2,1)} %reshape.243), calls=%async_computation | async-start | bytes 1048576 | tf_op jit(solution)/shard_map/all_to_all | solution.py:63
  31.3 13.8 %all-to-all-start.1 = ((bf16[8,2,16384]{2,1,0:T(2,128)(2,1)}), bf16[8,2,16384]{2,1,0:T(2,128)(2,1)S(1)}, u32[]{:S(2)}, u32[]{:S(2)}) async-start(bf16[8,2,16384]{2,1,0:T(2,128)(2,1)} %reshape.241), calls=%async_computation.1 | async-start | bytes 1048576 | tf_op jit(solution)/shard_map/all_to_all | solution.py:64
  35.5 141.5 %all-gather.2.cloned.1.call-start = ((), (), s32[]{:S(2)}) async-start(), calls=%async_computation.8 | async-start | bytes 4456448 | tf_op jit(solution)/shard_map/all_gather | solution.py:98
  45.7 3.5 copy-start
  87.3 5.4 copy-start.1
  87.3 43.5 %all-to-all-start.2 = ((bf16[8,2,81920]{2,1,0:T(2,128)(2,1)}), bf16[8,2,81920]{2,1,0:T(2,128)(2,1)}, u32[]{:S(2)}, u32[]{:S(2)}) async-start(bf16[8,2,81920]{2,1,0:T(2,128)(2,1)} %reshape.245), calls=%async_computation.2 | async-start | bytes 5242880 | tf_op jit(solution)/shard_map/all_to_all | solution.py:61
  130.8 6.4 %copy-start.2 = (bf16[1,256,8,128]{3,2,1,0:T(8,128)(2,1)S(1)}, bf16[1,256,8,128]{3,2,1,0:T(8,128)(2,1)}, u32[]{:S(2)}) copy-start(bf16[1,256,8,128]{3,2,1,0:T(8,128)(2,1)} %copy.137) | copy-start | bytes 1572868
  130.8 36.9 %all-to-all-start.3 = ((bf16[8,2,81920]{2,1,0:T(2,128)(2,1)}), bf16[8,2,81920]{2,1,0:T(2,128)(2,1)S(1)}, u32[]{:S(2)}, u32[]{:S(2)}) async-start(bf16[8,2,81920]{2,1,0:T(2,128)(2,1)} %reshape.247), calls=%async_computation.3 | async-start | bytes 5242880 | tf_op jit(solution)/shard_map/all_to_all | solution.py:62
  135.8 373.0 %reduce-scatter.2.cloned.1.call-start = ((), (), s32[]{:S(2)}) async-start(), calls=%async_computation.9 | async-start | bytes 4456448 | tf_op jit(solution)/shard_map/reduce_scatter | solution.py:203
  433.0 79.7 %all-to-all-start.4 = ((bf16[8,256,640]{1,2,0:T(8,128)(2,1)}), bf16[8,256,640]{1,2,0:T(8,128)(2,1)S(1)}, u32[]{:S(2)}, u32[]{:S(2)}) async-start(bf16[8,256,640]{1,2,0:T(8,128)(2,1)} %get-tuple-element.112), calls=%async_computation.4 | async-start | bytes 5242880 | tf_op jit(solution)/shard_map/all_to_all | solution.py:214
  512.8 16.2 %all-to-all-start.6 = ((bf16[8,256,128]{2,1,0:T(8,128)(2,1)}), bf16[8,256,128]{2,1,0:T(8,128)(2,1)S(1)}, u32[]{:S(2)}, u32[]{:S(2)}) async-start(bf16[8,256,128]{2,1,0:T(8,128)(2,1)} %copy.125), calls=%async_computation.7 | async-start | bytes 1048576 | tf_op jit(solution)/shard_map/all_to_all | solution.py:216
  529.0 14.5 %all-to-all-start.5 = ((bf16[8,256,128]{2,1,0:T(8,128)(2,1)}), bf16[8,256,128]{2,1,0:T(8,128)(2,1)}, u32[]{:S(2)}, u32[]{:S(2)}) async-start(bf16[8,256,128]{2,1,0:T(8,128)(2,1)} %copy.123), calls=%async_computation.6 | async-start | bytes 1048576 | tf_op jit(solution)/shard_map/all_to_all | solution.py:215
Sparse Core Ops, SparseCore 0:
  49.3 51.0 all-gather.1
  433.2 75.5 reduce-scatter.1
where the time goes:
time: 556 us; the launch traced here: 553 us
  local copies, waits for them, and re-layouts  183 us (33%)
  other arithmetic  116 us (21%)
  waiting for transfers between devices  111 us (20%)
  matrix products  57.4 us (10%)
  starting transfers between devices  37.5 us (7%)
  loops' own time  32.1 us (6%)
  between operations  14.3 us (3%)
    reduce_scatter x1, waiting for transfers between devices, body(): lax.psum_scatter(summed.reshape(PUB * lax.axis_size('seg'), slot_size, 2...  71.3 us
    dynamic_update_slice x40, local copies, waits for them, and re-layouts, body(): lax.map(segment_grads, (query_all, grad_all, stacked, local_rows(own_leng...  70.8 us
    unnamed x4, other arithmetic  60.7 us
    unnamed x36, local copies, waits for them, and re-layouts  54.2 us
    dynamic_slice x56, local copies, waits for them, and re-layouts, body(): lax.map(segment_grads, (query_all, grad_all, stacked, local_rows(own_leng...  33.4 us
    another operation x1, loops' own time, body(): lax.map(segment_grads, (query_all, grad_all, stacked, local_rows(own_leng...  32.1 us
    eq x8, other arithmetic, segment_grads(): column_block[None, :] == 0  19.9 us
    all_to_all x1, waiting for transfers between devices, body(): lax.all_to_all(grad_out, 'head', split_axis=2, concat_axis=0, tiled=True)  16.5 us
  transfers between devices with their start and end apart: 9, of which 6 were waited for; matrix products, arithmetic and copies ran while one was open for 22% of the time, Pallas kernels for 0%

commit v1 on v0

v1 whole, which is shorter than its diff:
```python
import jax
import jax.numpy as jnp
from jax import lax
from jax.experimental import pallas as pl
from jax.experimental.pallas import tpu as pltpu
from jax.sharding import PartitionSpec as P

DH = 128
PUB = 2
MESH = pl.DeviceIdType.MESH
SIDE = 4
NHEAD = 8
NCOL = 16
BF = jnp.bfloat16
F32 = jnp.float32
NEG = -1e30

T_PUB, T_ANC, T_ORDER, T_CONT, T_LAST, T_RANK, T_OWN = 0, 2, 18, 34, 50, 83, 91
T_SIZE = 96


def table_kernel(owners, parents, depths, lengths, out, inverse, shared):
    col = lax.axis_index("seg")
    mine = lax.axis_index("head")
    count = owners.shape[0]

    def invert(g, carry):
        inverse[owners[g]] = g
        return carry

    lax.fori_loop(0, count, invert, 0)

    def number(slot, rank):
        rank = jnp.where(slot % NHEAD == 0, 0, rank)
        g = inverse[slot]
        inner = g < NCOL * PUB

        @pl.when(inner)
        def _():
            shared[g] = (slot // NHEAD) * PUB + rank

        return rank + inner.astype(jnp.int32)

    lax.fori_loop(0, count, number, 0)
    targets = []
    rank = 0
    for p in range(NHEAD):
        g = inverse[col * NHEAD + p]
        inner = g < NCOL * PUB
        out[T_RANK + p] = jnp.where(inner, rank, 0)

        @pl.when(inner)
        def _():
            out[T_PUB + rank] = p

        rank = rank + inner.astype(jnp.int32)
        up = parents[g]
        depth = depths[g]
        one = (depth >= 1) & (up >= 0)
        up = jnp.maximum(up, 0)
        up2 = parents[up]
        two = (depth >= 2) & one & (up2 >= 0)
        up2 = jnp.maximum(up2, 0)
        first = shared[up]
        second = shared[up2]
        out[T_ANC + 2 * p] = jnp.where(one, first, 0)
        out[T_ANC + 2 * p + 1] = jnp.where(two, second, 0)
        targets.append(jnp.where(one, first, NCOL * PUB))
        targets.append(jnp.where(two, second, NCOL * PUB))

        @pl.when(p == mine)
        def _():
            out[T_OWN] = lengths[g]
            out[T_OWN + 1] = jnp.where(one, lengths[up], 0)
            out[T_OWN + 2] = jnp.where(two, lengths[up2], 0)
            out[T_OWN + 3] = inner.astype(jnp.int32)

    n = len(targets)
    places = [0] * n
    again = [False] * n
    for b in range(n):
        for a in range(b):
            c = targets[a] <= targets[b]
            places[b] = places[b] + c.astype(jnp.int32)
            places[a] = places[a] + 1 - c.astype(jnp.int32)
            again[b] = again[b] | (targets[a] == targets[b])
    for j in range(NCOL * PUB + 1):
        out[T_LAST + j] = n
    for l in range(n):
        out[T_ORDER + places[l]] = l
        out[T_CONT + places[l]] = jnp.int32(0) + again[l]
        out[T_LAST + targets[l]] = places[l]


def tables_of(owners, parents, depths, lengths):
    smem = pl.BlockSpec(memory_space=pltpu.SMEM)
    return pl.pallas_call(
        table_kernel,
        out_shape=jax.ShapeDtypeStruct((T_SIZE,), jnp.int32),
        in_specs=[smem] * 4,
        out_specs=smem,
        scratch_shapes=[pltpu.SMEM((128,), jnp.int32), pltpu.SMEM((32,), jnp.int32)],
    )(owners, parents, depths, lengths)


PEERS = [(0, 1), (1, 0), (3, 0), (1, 1), (3, 1), (2, 0), (2, 1)]


def kernel(tab, q_ref, k_ref, v_ref, g_ref, dq_ref, dk_ref, dv_ref,
           qv, gv, kown, vown, all_k, all_v, sh_k, sh_v, sel_k, sel_v, anc_k, anc_v,
           own_k, own_v, fb_k, fb_v, far_k, far_v, accs_k, accs_v, tt_k, tt_v,
           half_k, half_v, full_k, full_v, fin_k, fin_v, rb_k, rb_v, ret_k, ret_v,
           dqv, bias, live, kc, vc, kt, send_sem, recv_sem, local_sem, out_sem):
    seg = lax.axis_index("seg")
    head = lax.axis_index("head")
    slot = qv.shape[0]
    mid = slot // 2
    y, x = seg // SIDE, seg % SIDE
    z, core = head // 2, head % 2

    def peer(step):
        dz, dc = step
        return ((z + dz) % SIDE) * 2 + (core + dc) % 2

    def along(axis, step):
        if axis == 0:
            return y * SIDE + (x + step) % SIDE
        return ((y + step) % SIDE) * SIDE + x

    def at(axis, da, db):
        if axis == 0:
            return ((y + db) % SIDE) * SIDE + (x + da) % SIDE
        return ((y + da) % SIDE) * SIDE + (x + db) % SIDE

    ids = [0]
    sent = []

    def push(src, dst, to_seg, to_head):
        n = ids[0]
        ids[0] += 1
        copy = pltpu.make_async_remote_copy(
            src_ref=src, dst_ref=dst, send_sem=send_sem.at[n], recv_sem=recv_sem.at[n],
            device_id=(to_seg, to_head), device_id_type=MESH)
        copy.start()
        sent.append(copy)
        return copy

    barrier = pltpu.get_barrier_semaphore()
    for step in PEERS:
        pl.semaphore_signal(barrier, inc=1, device_id=(seg, peer(step)), device_id_type=MESH)
    for axis in (0, 1):
        for step in (1, 3):
            pl.semaphore_signal(barrier, inc=1, device_id=(along(axis, step), head), device_id_type=MESH)
    pl.semaphore_wait(barrier, len(PEERS) + 4)

    def lanes(p):
        return pl.ds(pl.multiple_of(p * DH, DH), DH)

    first = [[], []]
    for kv, (src, dst) in enumerate(((k_ref, all_k), (v_ref, all_v))):
        for step in PEERS:
            p = peer(step)
            first[kv].append(push(src.at[0, :, lanes(p)], dst.at[head], seg, p))
    loads = [
        pltpu.make_async_copy(src.at[0], dst, local_sem.at[n])
        for n, (src, dst) in enumerate(((k_ref, kown), (v_ref, vown), (q_ref, qv), (g_ref, gv)))
    ]
    for load in loads:
        load.start()

    length = tab[T_OWN]
    rows = lax.broadcasted_iota(jnp.int32, (slot, slot), 0)
    cols = lax.broadcasted_iota(jnp.int32, (slot, slot), 1)
    bias[0:slot, :] = jnp.where((rows <= cols) & (rows < length), 0.0, NEG)
    bias[slot:2 * slot, :] = jnp.where(rows < tab[T_OWN + 1], 0.0, NEG)
    bias[2 * slot:3 * slot, :] = jnp.where(rows < tab[T_OWN + 2], 0.0, NEG)
    row = lax.broadcasted_iota(jnp.int32, (slot, DH), 0)
    live[...] = jnp.where(row < length, 1.0, 0.0).astype(BF)

    class Gather:
        def __init__(self, sh, whole, own, arrived):
            self.sh, self.whole, self.own, self.arrived = sh, whole, own, arrived

        def block(self, r, da, db, part=None):
            ref = self.sh.at[at(r, da, db) * PUB + r]
            if part is None:
                return ref
            return ref.at[pl.ds(part * mid, mid)]

        def spread(self, r, axis, da, db):
            ref = self.block(r, da, db)
            return [push(ref, ref, along(axis, 1), head), push(ref, ref, along(axis, 3), head)]

        def relay(self, r, axis, da, db, pair):
            out = []
            for part, copy in enumerate(pair):
                copy.wait_recv()
                step = 3 if part == 0 else 1
                ref = self.block(r, step if axis == r else da, db if axis == r else step, part)
                out.append(push(ref, ref, along(axis, 1 if part == 0 else 3), head))
            return out

        def steps(self):
            for copy in self.arrived:
                copy.wait_recv()
            self.whole[head] = self.own[:, lanes(head)]
            for r in range(PUB):
                self.sh[seg * PUB + r] = self.whole[tab[T_PUB + r]]
            a, b, fa, fb = {}, {}, {}, {}
            for r in range(PUB):
                a[r] = self.spread(r, r, 0, 0)
                b[r, 0] = self.spread(r, 1 - r, 0, 0)
            yield
            for r in range(PUB):
                fa[r] = self.relay(r, r, 0, 0, a[r])
                b[r, 3] = self.spread(r, 1 - r, 3, 0)
                b[r, 1] = self.spread(r, 1 - r, 1, 0)
            yield
            for r in range(PUB):
                fb[r, 0] = self.relay(r, 1 - r, 0, 0, b[r, 0])
            yield
            for r in range(PUB):
                for copy in fa[r]:
                    copy.wait_recv()
                b[r, 2] = self.spread(r, 1 - r, 2, 0)
            for r in range(PUB):
                for da in (3, 1):
                    fb[r, da] = self.relay(r, 1 - r, da, 0, b[r, da])
            yield
            for r in range(PUB):
                fb[r, 2] = self.relay(r, 1 - r, 2, 0, b[r, 2])
            yield
            for pair in fb.values():
                for copy in pair:
                    copy.wait_recv()

    def run(seq):
        for _ in seq:
            return True
        return False

    def select(sh, sel, anc):
        out = {}
        for step in PEERS:
            p = peer(step)
            for a in range(2):
                sel[p * 2 + a] = sh[tab[T_ANC + 2 * p + a]]
            out[step] = push(sel.at[pl.ds(p * 2, 2)], anc.at[pl.ds(head * 2, 2)], seg, p)
        for a in range(2):
            anc[head * 2 + a] = sh[tab[T_ANC + 2 * head + a]]
        return out

    loads[0].wait()
    loads[1].wait()
    gather_k = Gather(sh_k, all_k, kown, first[0]).steps()
    gather_v = Gather(sh_v, all_v, vown, first[1]).steps()
    run(gather_k)
    run(gather_k)
    run(gather_v)
    run(gather_k)
    run(gather_v)
    run(gather_k)
    run(gather_v)
    run(gather_k)
    run(gather_v)
    run(gather_k)
    got_k = select(sh_k, sel_k, anc_k)
    run(gather_v)
    run(gather_v)
    got_v = select(sh_v, sel_v, anc_v)
    loads[2].wait()
    loads[3].wait()

    group = qv.shape[1] // kown.shape[1]
    scale = DH ** -0.5
    exp_scale = scale * 1.4426950408889634
    nt = (((1,), (1,)), ((), ()))
    back = []
    writes = []
    for n, step in enumerate([(0, 0)] + PEERS):
        p = peer(step)
        if n > 0:
            away = ((SIDE - step[0]) % SIDE, step[1])
            got_k[away].wait_recv()
            got_v[away].wait_recv()
        kc[0:slot] = kown[:, lanes(p)]
        vc[0:slot] = vown[:, lanes(p)]
        for a in range(2):
            kc[(a + 1) * slot:(a + 2) * slot] = anc_k[p * 2 + a]
            vc[(a + 1) * slot:(a + 2) * slot] = anc_v[p * 2 + a]
        kt[...] = kc[...].T

        def one(j, carry, p=p):
            dk, dv = carry
            place = lanes(p * group + j)
            q = qv[:, place]
            g = gv[:, place] * live[...]
            s = lax.dot_general(kc[...], q, nt, preferred_element_type=F32) * exp_scale + bias[...]
            top = jnp.max(s, axis=0, keepdims=True)
            e = jnp.exp2(s - top)
            inv = 1.0 / jnp.sum(e, axis=0, keepdims=True)
            wg = lax.dot_general(vc[...], g, nt, preferred_element_type=F32)
            delta = jnp.sum(e * wg, axis=0, keepdims=True) * inv
            ds = (e * (wg - delta)).astype(BF)
            inv_col = jnp.broadcast_to(inv, (DH, slot)).T
            g = (g.astype(F32) * inv_col).astype(BF)
            q = (q.astype(F32) * inv_col).astype(BF)
            dv = dv + jnp.dot(e.astype(BF), g, preferred_element_type=F32)
            dk = dk + jnp.dot(ds, q, preferred_element_type=F32)
            dqt = jnp.dot(kt[...], ds, preferred_element_type=F32) * (inv * scale)
            dqv[:, place] = dqt.T.astype(BF)
            return dk, dv

        zero = jnp.zeros((3 * slot, DH), F32)
        dk, dv = lax.fori_loop(0, group, one, (zero, zero))
        dk = dk * scale
        own_k[p] = dk[0:slot]
        own_v[p] = dv[0:slot]
        wide = pl.ds(pl.multiple_of(p * (group * DH), DH), group * DH)
        write = pltpu.make_async_copy(dqv.at[:, wide], dq_ref.at[0, :, wide], out_sem.at[n])
        write.start()
        writes.append(write)
        fk, fv = (far_k, far_v) if n == 0 else (fb_k, fb_v)
        for a in range(2):
            fk[p * 2 + a] = dk[(a + 1) * slot:(a + 2) * slot].astype(BF)
            fv[p * 2 + a] = dv[(a + 1) * slot:(a + 2) * slot].astype(BF)
        if n > 0:
            back.append(push(fb_k.at[pl.ds(p * 2, 2)], far_k.at[pl.ds(head * 2, 2)], seg, p))
            back.append(push(fb_v.at[pl.ds(p * 2, 2)], far_v.at[pl.ds(head * 2, 2)], seg, p))

    for copy in back:
        copy.wait_recv()
    links = 2 * NHEAD

    def sums(far, accs, tt):
        def add(n, acc):
            acc = far[tab[T_ORDER + n]].astype(F32) + acc * tab[T_CONT + n].astype(F32)
            accs[n] = acc.astype(BF)
            return acc

        lax.fori_loop(0, links, add, jnp.zeros((slot, DH), F32))
        accs[links] = jnp.zeros((slot, DH), BF)

        def spread(j, carry):
            tt[j] = accs[tab[T_LAST + j]]
            return carry

        lax.fori_loop(0, NCOL * PUB, spread, 0)

    def plus(*terms):
        total = terms[0].astype(F32)
        for term in terms[1:]:
            total = total + term.astype(F32)
        return total.astype(BF)

    class Scatter:
        def __init__(self, far, accs, tt, half, full, fin):
            self.far, self.accs, self.tt = far, accs, tt
            self.half, self.full, self.fin = half, full, fin

        def block(self, r, axis, da, db):
            return self.tt.at[at(axis, da, db) * PUB + r]

        def send_far(self, r, axis, other, slot_no):
            ref = self.block(r, axis, 2, other)
            out = []
            for part, step in ((0, 1), (1, 3)):
                out.append(push(ref.at[pl.ds(part * mid, mid)], self.half.at[(r * 5 + slot_no) * 2 + part],
                                along(axis, step), head))
            return out

        def send_near(self, r, axis, other, slot_no, pair):
            out = []
            for part, step in ((0, 1), (1, 3)):
                pair[part].wait_recv()
                ref = self.block(r, axis, step, other)
                span = pl.ds(part * mid, mid)
                ref[span] = plus(ref[span], self.half[(r * 5 + slot_no) * 2 + part])
                out.append(push(ref, self.full.at[(r * 5 + slot_no) * 2 + part], along(axis, step), head))
            return out

        def total(self, r, axis, other, slot_no, pair):
            for copy in pair:
                copy.wait_recv()
            ref = self.block(r, axis, 0, other)
            n = (r * 5 + slot_no) * 2
            return ref, plus(ref[...], self.full[n], self.full[n + 1])

        def steps(self):
            sums(self.far, self.accs, self.tt)
            a, b = {}, {}
            for r in range(PUB):
                for other in (2, 1, 3, 0):
                    a[r, other] = self.send_far(r, 1 - r, other, other)
            yield
            for other in (2, 1, 3, 0):
                for r in range(PUB):
                    b[r, other] = self.send_near(r, 1 - r, other, other, a[r, other])
            yield
            for r in range(PUB):
                ref, value = self.total(r, 1 - r, 2, 2, b[r, 2])
                ref[...] = value
                a[r] = self.send_far(r, r, 0, 4)
            yield
            for other in (1, 3):
                for r in range(PUB):
                    ref, value = self.total(r, 1 - r, other, other, b[r, other])
                    ref[...] = value
            for r in range(PUB):
                b[r] = self.send_near(r, r, 0, 4, a[r])
            yield
            for r in range(PUB):
                ref, value = self.total(r, 1 - r, 0, 0, b[r, 0])
                ref[...] = value
            for r in range(PUB):
                ref, value = self.total(r, r, 0, 4, b[r])
                self.fin[r] = value

    def give(fin, rb, ret):
        out = []
        for step in PEERS:
            p = peer(step)
            rb[p] = fin[tab[T_RANK + p]]
            out.append(push(rb.at[p], ret.at[head], seg, p))
        ret[head] = fin[tab[T_RANK + head]]
        return out

    scatter_k = Scatter(far_k, accs_k, tt_k, half_k, full_k, fin_k).steps()
    scatter_v = Scatter(far_v, accs_v, tt_v, half_v, full_v, fin_v).steps()
    run(scatter_k)
    run(scatter_v)
    run(scatter_k)
    run(scatter_k)
    run(scatter_v)
    run(scatter_k)
    run(scatter_v)
    run(scatter_k)
    give_k = give(fin_k, rb_k, ret_k)
    run(scatter_v)
    run(scatter_v)
    give_v = give(fin_v, rb_v, ret_v)
    inner = tab[T_OWN + 3] > 0

    for copies, own, ret, out in ((give_k, own_k, ret_k, dk_ref), (give_v, own_v, ret_v, dv_ref)):
        for copy in copies:
            copy.wait_recv()
        for p in range(NHEAD):
            out[0, :, p * DH:(p + 1) * DH] = (
                own[p] + jnp.where(inner, ret[p].astype(F32), 0.0)).astype(BF)

    for copy in sent:
        copy.wait_send()
    for write in writes:
        write.wait()


def body(queries, key_states, values, grad_out, owners, parents, depths, lengths):
    tab = tables_of(owners, parents, depths, lengths)
    _, slot, width = queries.shape
    kv_width = key_states.shape[2]
    any_space = pl.BlockSpec(memory_space=pl.ANY)
    vmem = pl.BlockSpec(memory_space=pltpu.VMEM)

    def blocks(n, rows=slot, dtype=BF):
        return [pltpu.VMEM((n, rows, DH), dtype)] * 2

    scratch = (
        [pltpu.VMEM((slot, width), BF)] * 2
        + [pltpu.VMEM((slot, kv_width), BF)] * 2
        + blocks(NHEAD)
        + blocks(NCOL * PUB)
        + blocks(2 * NHEAD)
        + blocks(2 * NHEAD)
        + blocks(NHEAD, dtype=F32)
        + blocks(2 * NHEAD)
        + blocks(2 * NHEAD)
        + blocks(2 * NHEAD + 1)
        + blocks(NCOL * PUB)
        + blocks(PUB * 5 * 2, slot // 2)
        + blocks(PUB * 5 * 2)
        + blocks(PUB)
        + blocks(NHEAD)
        + blocks(NHEAD)
        + [
            pltpu.VMEM((slot, width), BF),
            pltpu.VMEM((3 * slot, slot), F32),
            pltpu.VMEM((slot, DH), BF),
            pltpu.VMEM((3 * slot, DH), BF),
            pltpu.VMEM((3 * slot, DH), BF),
            pltpu.VMEM((DH, 3 * slot), BF),
            pltpu.SemaphoreType.DMA((216,)),
            pltpu.SemaphoreType.DMA((216,)),
            pltpu.SemaphoreType.DMA((4,)),
            pltpu.SemaphoreType.DMA((NHEAD,)),
        ]
    )
    return pl.pallas_call(
        kernel,
        out_shape=(
            jax.ShapeDtypeStruct(queries.shape, BF),
            jax.ShapeDtypeStruct(key_states.shape, BF),
            jax.ShapeDtypeStruct(values.shape, BF),
        ),
        in_specs=[pl.BlockSpec(memory_space=pltpu.SMEM)] + [any_space] * 4,
        out_specs=(any_space, vmem, vmem),
        scratch_shapes=scratch,
        compiler_params=pltpu.CompilerParams(
            collective_id=0, has_side_effects=True, vmem_limit_bytes=60 * 2**20),
        cost_estimate=pl.CostEstimate(
            flops=10 * QH_FLOPS * slot, bytes_accessed=10 * 2**20, transcendentals=slot * 3 * slot * width // DH),
    )(tab, queries, key_states, values, grad_out)


QH_FLOPS = 40 * 768 * 128


def solution(mesh):
    placed = (P(("seg", "head"), None, None),) * 4 + (P(),) * 4
    return jax.shard_map(
        body,
        mesh=mesh,
        in_specs=placed,
        out_specs=(P(("seg", "head"), None, None),) * 3,
        check_vma=False,
    )
```

time: 556 us -> 151 us (0.27)
  local copies, waits for them, and re-layouts: 183 us -> 5.08 us
  Pallas kernels: 0 us -> 145 us
  other arithmetic: 116 us -> 0 us
  waiting for transfers between devices: 111 us -> 0 us
  matrix products: 57.4 us -> 0 us
  starting transfers between devices: 37.5 us -> 0 us
  loops' own time: 32.1 us -> 0 us
  between operations: 14.3 us -> 0.67 us
    pallas_call x0 -> x2, Pallas kernels: none -> 145 us  [the longest x1 140 us: body(): pl.pallas_call(kernel, out_shape=(jax.ShapeDtypeStruct(queries.shape, BF)...]
    reduce_scatter x1 -> x0, waiting for transfers between devices: 71.3 us -> none  [body(): lax.psum_scatter(summed.reshape(PUB * lax.axis_size('seg'), slot_size, 2...]
    dynamic_update_slice x40 -> x0, local copies, waits for them, and re-layouts: 70.8 us -> none  [body(): lax.map(segment_grads, (query_all, grad_all, stacked, local_rows(own_leng...]
    unnamed x4 -> x0, other arithmetic: 60.7 us -> none
    dot_general x51 -> x0, matrix products: 57.4 us -> none  [the longest x8 10.5 us: segment_grads(): jnp.einsum('tkgd,ukd->kgtu', gated, value_cat, preferred_element_type=jnp...]
    unnamed x36 -> x7, local copies, waits for them, and re-layouts: 54.2 us -> 5.08 us
    all_to_all x7 -> x0, waiting for transfers between devices: 40.1 us -> none  [the longest x1 16.5 us: body(): lax.all_to_all(grad_out, 'head', split_axis=2, concat_axis=0, tiled=True)]
    all_to_all x7 -> x0, starting transfers between devices: 37.5 us -> none  [the longest x1 6.81 us: body(): lax.all_to_all(key_states, 'head', split_axis=2, concat_axis=0, tiled=True)]
  transfers between devices with their start and end apart: 9 -> 0, of which waited for: 6 -> 0; matrix products, arithmetic and copies ran while one was open for 22% -> 0% of each run, Pallas kernels for 0% -> 0%
where the time goes in v1:
time: 151 us
  Pallas kernels  145 us (96%)
  local copies, waits for them, and re-layouts  5.08 us (3%)
    pallas_call x1, Pallas kernels, body(): pl.pallas_call(kernel, out_shape=(jax.ShapeDtypeStruct(queries.shape, BF)...  140 us
    unnamed x7, local copies, waits for them, and re-layouts  5.08 us
    pallas_call x1, Pallas kernels, tables_of(): pl.pallas_call(table_kernel, out_shape=jax.ShapeDtypeStruct((T_SIZE,), jn...  4.47 us

profile of v1, /device:TPU:1, one launch (start us, length us, event | category | flops | bytes accessed | tf_op | source)
XLA Modules:
  0.0 150.7 jit_solution(10312971449633376626)
XLA Ops:
  0.6 4.5 %shard_map.103.tab = s32[96]{0:T(128)} custom-call(s32[128]{0:T(128)} %owners.1, s32[128]{0:T(128)} %parents.1, s32[128]{0:T(128)} %depths.1, s32[128]{0:T(128)} %lengths.1), custom_call_target="tpu_custom_call" | custom-call | tf_op jit(solution)/shard_map/pallas_call | solution.py:97
  5.1 140.5 %shard_map.104 = (bf16[1,256,5120]{2,1,0:T(8,128)(2,1)}, bf16[1,256,1024]{2,1,0:T(8,128)(2,1)}, bf16[1,256,1024]{2,1,0:T(8,128)(2,1)}) custom-call(s32[96]{0:T(128)} %shard_map.103.tab, bf16[1,256,5120]{2,1,0:T(8,128)(2,1)} %q_ref.1, bf16[1,256,1024]{2,1,0:T(8,128)(2,1)} %k_ref.1, bf16[1,256,1024]{2,1,0:T(8,128)(2,1)} %v_ref.1, bf16[1,256,5120]{2,1,0:T(8,128)(2,1)} %g_ref.1), custom_call_target="tpu_custom_call" | custom-call | flops 10066329600 | bytes 10485760 | tf_op jit(solution)/shard_map/pallas_call | solution.py:497
  145.6 0.0 copy-start.1
  145.6 0.0 copy-start
  145.6 3.5 %copy.14 = bf16[1,256,5120]{2,1,0:T(8,128)(2,1)} copy(bf16[1,256,5120]{2,1,0:T(8,128)(2,1)} %get-tuple-element.6) | data formatting | bytes 5242880
  149.1 0.0 copy-done.1
  149.1 0.8 copy.15
  149.9 0.0 copy-done
  149.9 0.8 copy.16
Async XLA Ops:
  145.6 3.5 %copy-start.1 = (bf16[1,256,1024]{2,1,0:T(8,128)(2,1)S(1)}, bf16[1,256,1024]{2,1,0:T(8,128)(2,1)}, u32[]{:S(2)}) copy-start(bf16[1,256,1024]{2,1,0:T(8,128)(2,1)} %get-tuple-element.7) | copy-start | bytes 1572868
  145.6 4.3 %copy-start = (bf16[1,256,1024]{2,1,0:T(8,128)(2,1)S(1)}, bf16[1,256,1024]{2,1,0:T(8,128)(2,1)}, u32[]{:S(2)}) copy-start(bf16[1,256,1024]{2,1,0:T(8,128)(2,1)} %get-tuple-element.8) | copy-start | bytes 1572868
